TPU v7x, 512 devices: a whole 4x8x8 slice. The times are simulated.
512 devices in a mesh: ctx: 16 (over z_lo, y), exp: 32 (over x, z_hi, core).
Axes of the slice: x: 4, y: 8, z: 8 (z_hi: 4, z_lo: 2; z = z_hi * 2 + z_lo), core: 2. Of those that a mesh axis runs over, the one named last changes fastest.
Arguments:
- queries: bfloat16 [2048, 8192], P('ctx', 'exp'), may hold values from -6 to 6
- keys: bfloat16 [2048, 512], P('ctx'), may hold values from -6 to 6
- values: bfloat16 [2048, 512], P('ctx'), may hold values from -5 to 5
- residual: bfloat16 [2048, 4096], P(('ctx', 'exp')), may hold values from -6 to 6
- out_weight: bfloat16 [8192, 4096], P('exp'), may hold values from -0.125 to 0.125
- norm_gain: float32 [4096], replicated, may hold values from 0.25 to 1.75
- expert_ids: int32 [2048, 8], P(('ctx', 'exp')), may hold values from 0 to 31, all different within a row; in each aligned block of 4 rows (0 to 3, 4 to 7, ...) at most 2 rows name the same one
- expert_gates: float32 [2048, 8], P(('ctx', 'exp')), may hold values from 0.05 to 0.35
- w_gate: bfloat16 [32, 4096, 1536], P('exp', None, 'ctx'), may hold values from -0.09375 to 0.09375
- w_up: bfloat16 [32, 4096, 1536], P('exp', None, 'ctx'), may hold values from -0.09375 to 0.09375
- w_down: bfloat16 [32, 1536, 4096], P('exp', None, 'ctx'), may hold values from -0.3125 to 0.3125
Outputs:
- mixed: bfloat16 [2048, 4096], P(('ctx', 'exp'))
- experts_out: bfloat16 [2048, 4096], P(('ctx', 'exp'))
Inputs may be any that keep to these rules, and one draw needn't show every extreme that they name: `expert_ids`: in each aligned block of 4 rows (the rows of one device) no expert is named by more than 2 rows, a bound that some block reaches.
All inputs are finite; a program needn't handle non-finite values.
Results may differ from a plain program's by a relative error of at most 0.034.
Values may be sent and summed in bfloat16 or wider, within the bound.
No kernel may reach another device: no remote copies, remote signals or barrier semaphores. Data moves between devices by JAX's collectives and lax.ppermute only.
A program may use at most 64 MiB of HBM per device.

v0:
```python
import jax
import jax.numpy as jnp
import numpy as np
from jax import lax
from jax.sharding import Mesh, PartitionSpec as P

HEAD_WIDTH = 128
EXTRA = 128
CTX = ("zl", "y")
EXP = ("x", "zh", "co")
EPS_NORM = 1e-06
NEG_LARGE = -1e30


def exchange(pieces, axis):
    return lax.all_to_all(pieces, axis, 0, 0, tiled=True)


def spread(value, axis, count):
    return exchange(jnp.broadcast_to(value[None], (count,) + value.shape), axis)


def added(pieces):
    return jnp.sum(pieces.astype(jnp.float32), axis=0)


def rows_dot(left, right):
    return lax.dot_general(
        left, right, (((1,), (1,)), ((), ())), preferred_element_type=jnp.float32
    )


def route(expert_ids, expert_gates, expert_count, slots):
    flat_ids = expert_ids.reshape(-1)
    tok_rows, top_count = expert_ids.shape
    owner_row = jnp.arange(tok_rows * top_count, dtype=jnp.int32) // top_count
    earlier = (flat_ids[:, None] == flat_ids[None, :]) & (owner_row[None, :] < owner_row[:, None])
    slot_ids = jnp.sum(earlier.astype(jnp.int32), axis=1).reshape(tok_rows, top_count)
    expert_hit = (
        expert_ids[None, None] == jnp.arange(expert_count, dtype=jnp.int32)[:, None, None, None]
    )
    slot_hit = slot_ids[None, None] == jnp.arange(slots, dtype=jnp.int32)[None, :, None, None]
    hits = expert_hit & slot_hit
    table = jnp.any(hits, axis=3).astype(jnp.bfloat16)
    mix = jnp.sum(jnp.where(hits, expert_gates[None, None], 0.0), axis=3)
    return (
        table.reshape(expert_count * slots, tok_rows),
        mix.reshape(expert_count * slots, tok_rows),
    )


def on_device(
    queries,
    keys,
    values,
    residual,
    out_weight,
    norm_gain,
    expert_ids,
    expert_gates,
    w_gate,
    w_up,
    w_down,
):
    n_zl, n_y = (lax.axis_size("zl"), lax.axis_size("y"))
    n_x, n_zh, n_co = (lax.axis_size("x"), lax.axis_size("zh"), lax.axis_size("co"))
    zl, y_pos, x_pos, co = (lax.axis_index(a) for a in ("zl", "y", "x", "co"))
    ctx_count, expert_count = (n_zl * n_y, n_x * n_zh * n_co)
    width = residual.shape[1]
    tok_dev, top_count = expert_ids.shape
    slots = 2
    tok_block = queries.shape[0]
    heads = queries.shape[1] // HEAD_WIDTH
    swap = [(i, n_zl - 1 - i) for i in range(n_zl)]
    gate_up = jnp.stack([w_gate[0].T, w_up[0].T])
    gate_up_other = lax.ppermute(gate_up, "zl", swap)
    down_other = lax.ppermute(w_down[0], "zl", swap)
    mine = jnp.where(co == 0, keys, values)
    mine = lax.dynamic_slice_in_dim(mine, x_pos * HEAD_WIDTH, HEAD_WIDTH, 1)
    gathered = spread(mine, CTX, ctx_count).reshape(ctx_count * tok_block, HEAD_WIDTH)
    key_all, value_all = spread(gathered, "co", n_co)
    order = np.arange(tok_block).reshape(n_x, n_zh, n_co, tok_dev).transpose(2, 0, 1, 3)
    split = queries.reshape(n_x, n_zh, n_co, tok_dev, heads, HEAD_WIDTH)
    query_rows = jnp.transpose(split, (4, 2, 0, 1, 3, 5)).reshape(heads * tok_block, HEAD_WIDTH)
    query_pos = (zl * n_y + y_pos) * tok_block + jnp.asarray(
        np.tile(order.reshape(-1), heads), jnp.int32
    )
    key_pos = jnp.arange(key_all.shape[0], dtype=jnp.int32)
    allowed = key_pos[None, :] <= query_pos[:, None]
    scores = rows_dot(query_rows, key_all) * (1.0 / HEAD_WIDTH**0.5)
    scores = jnp.where(allowed, scores, NEG_LARGE)
    weights = jnp.exp(scores - jnp.max(scores, axis=1, keepdims=True))
    total = jnp.sum(weights, axis=1, keepdims=True)
    numer = jnp.dot(weights.astype(jnp.bfloat16), value_all, preferred_element_type=jnp.float32)
    done = (numer / total).astype(jnp.bfloat16).reshape(heads, tok_block, HEAD_WIDTH)
    heads_out = jnp.transpose(done, (1, 0, 2)).reshape(tok_block, heads * HEAD_WIDTH)
    partial = jnp.dot(heads_out, out_weight, preferred_element_type=jnp.float32)
    partial = partial.astype(jnp.bfloat16).reshape(n_co, tok_block // n_co, width)
    partial = added(exchange(partial, "co")).astype(jnp.bfloat16)
    projected = added(exchange(partial.reshape(n_x * n_zh, tok_dev, width), ("x", "zh")))
    mixed = (residual.astype(jnp.float32) + projected).astype(jnp.bfloat16)
    stream = mixed.astype(jnp.float32)
    mean_sq = jnp.mean(stream * stream, axis=1, keepdims=True)
    normed = (stream * lax.rsqrt(mean_sq + EPS_NORM) * norm_gain[None, :]).astype(jnp.bfloat16)
    table, mix = route(expert_ids, expert_gates, expert_count, slots)
    mix_high = mix.astype(jnp.bfloat16)
    mix_low = (mix - mix_high.astype(jnp.float32)).astype(jnp.bfloat16)
    extra = jnp.concatenate([mix_high, mix_low], axis=1)
    extra = jnp.pad(extra, ((0, 0), (0, EXTRA - extra.shape[1])))
    outgoing = jnp.dot(table, normed, preferred_element_type=jnp.float32).astype(jnp.bfloat16)
    outgoing = jnp.concatenate([outgoing, extra], axis=1)
    arrived = exchange(outgoing.reshape(expert_count, slots, width + EXTRA), EXP)
    rows = lax.all_gather(
        arrived.reshape(expert_count * slots, width + EXTRA), "y", axis=0, tiled=True
    )
    weight_in = jnp.stack([gate_up, gate_up_other], axis=1)
    weight_in = jnp.pad(weight_in, ((0, 0),) * 3 + ((0, EXTRA),)).reshape(-1, width + EXTRA)
    both = rows_dot(weight_in, rows)
    units = both.shape[0] // 2
    hidden = (jax.nn.silu(both[:units]) * both[units:]).astype(jnp.bfloat16)
    hidden = spread(hidden, "y", n_y).reshape(n_y * units, -1)
    down = jnp.concatenate([w_down[0], down_other], axis=1)
    down = down.reshape(n_zl, n_y, units // n_zl, down.shape[1])
    down = jnp.where(zl == 0, down, down[::-1])
    down = jnp.transpose(down, (1, 0, 2, 3)).reshape(n_y * units, -1)
    result = lax.dot_general(
        hidden, down, (((0,), (0,)), ((), ())), preferred_element_type=jnp.float32
    )
    gates = rows[:, width : width + 2 * tok_dev].astype(jnp.float32)
    gates = gates[:, :tok_dev] + gates[:, tok_dev:]
    result = (result * jnp.sum(gates, axis=1, keepdims=True)).astype(jnp.bfloat16)
    block_of = np.arange(n_y * expert_count).reshape(n_y, n_x, n_zh, n_co)
    block_of = block_of.transpose(3, 1, 2, 0).reshape(-1)
    token_of = (block_of[:, None] * tok_dev + np.arange(tok_dev)[None, :]).reshape(-1)
    place = jnp.sum(
        (gates != 0).astype(jnp.int32) * jnp.arange(1, tok_dev + 1, dtype=jnp.int32)[None, :],
        axis=1,
    )
    slot_block = jnp.arange(n_y * expert_count * slots, dtype=jnp.int32) // slots
    slot_token = jnp.where(place > 0, slot_block * tok_dev + place - 1, -1)
    onehot = (jnp.asarray(token_of, jnp.int32)[:, None] == slot_token[None, :]).astype(jnp.bfloat16)
    tokens = jnp.dot(onehot, result, preferred_element_type=jnp.float32).astype(jnp.bfloat16)
    cols = tokens.shape[1]
    tokens = added(exchange(tokens.reshape(n_co, -1, cols), "co")).astype(jnp.bfloat16)
    tokens = added(exchange(tokens.reshape(n_x, -1, cols), "x")).astype(jnp.bfloat16)
    tokens = exchange(tokens.reshape(n_zh * n_y, tok_dev, cols), ("zh", "y"))
    tokens = added(tokens.reshape(n_zh, n_y, tok_dev, cols))
    tokens = tokens.reshape(n_y, tok_dev, n_zl, cols // n_zl).transpose(1, 2, 0, 3)
    tokens = jnp.where(zl == 0, tokens, tokens[:, ::-1])
    return (mixed, tokens.reshape(tok_dev, width).astype(jnp.bfloat16))


def solution(mesh):
    fine = Mesh(mesh.devices.reshape(2, 8, 4, 4, 2), CTX + EXP)
    return jax.shard_map(
        on_device,
        mesh=fine,
        in_specs=(
            P(CTX, EXP),
            P(CTX, None),
            P(CTX, None),
            P(CTX + EXP, None),
            P(EXP, None),
            P(),
            P(CTX + EXP, None),
            P(CTX + EXP, None),
            P(EXP, None, CTX),
            P(EXP, None, CTX),
            P(EXP, None, CTX),
        ),
        out_specs=(P(CTX + EXP, None), P(CTX + EXP, None)),
        check_vma=False,
    )
```

profile of v0, /device:TPU:8, one launch (start us, length us, event | category | flops | bytes accessed | tf_op | source)
XLA Modules:
  0.0 259.2 jit_solution(8927563244535573260)
XLA Ops:
  7.2 0.9 dynamic-slice_select_fusion
  8.1 0.9 broadcast_in_dim.21
  9.0 9.4 %all-to-all-start = ((bf16[16,128,128]{2,1,0:T(8,128)(2,1)}), bf16[16,128,128]{2,1,0:T(8,128)(2,1)S(1)}, u32[]{:S(2)}, u32[]{:S(2)}) async-start(bf16[16,128,128]{2,1,0:T(8,128)(2,1)} %broadcast_in_dim.21), calls=%async_computation | async-start | bytes 1048576 | tf_op jit(solution)/shard_map/all_to_all | solution.py:16
  18.4 0.9 reshape.150
  21.0 12.4 %all-to-all-done = bf16[16,128,128]{2,1,0:T(8,128)(2,1)S(1)} async-done(((bf16[16,128,128]{2,1,0:T(8,128)(2,1)}), bf16[16,128,128]{2,1,0:T(8,128)(2,1)S(1)}, u32[]{:S(2)}, u32[]{:S(2)}) %all-to-all-start) | async-done | bytes 524320 | tf_op jit(solution)/shard_map/all_to_all | solution.py:16
  33.4 4.6 %all_to_all.45 = bf16[2,2048,128]{2,1,0:T(8,128)(2,1)S(1)} all-to-all(bf16[2,2048,128]{2,1,0:T(8,128)(2,1)S(1)} %broadcast_in_dim.23), channel_id=1, replica_groups=mesh['zl'=2,'y'=8,'x'=4,'zh'=4,'co'=2] {'co'}, dimensions={0} | all-to-all | bytes 2097152 | tf_op jit(solution)/shard_map/all_to_all | solution.py:16
  40.0 4.6 %all_to_all.46 = bf16[2,64,4096]{2,1,0:T(8,128)(2,1)S(1)} all-to-all(bf16[2,64,4096]{2,1,0:T(8,128)(2,1)S(1)} %bitcast.69), channel_id=1, replica_groups=mesh['zl'=2,'y'=8,'x'=4,'zh'=4,'co'=2] {'co'}, dimensions={0} | all-to-all | bytes 2097152 | tf_op jit(solution)/shard_map/all_to_all | solution.py:16
  44.6 1.1 reduce_sum.109
  45.7 2.0 reshape.155
  47.8 12.0 %all-to-all-start.3 = ((bf16[16,4,4096]{2,1,0:T(4,128)(2,1)}), bf16[16,4,4096]{2,1,0:T(4,128)(2,1)S(1)}, u32[]{:S(2)}, u32[]{:S(2)}) async-start(bf16[16,4,4096]{2,1,0:T(4,128)(2,1)} %reshape.155), calls=%async_computation.3 | async-start | bytes 1048576 | tf_op jit(solution)/shard_map/all_to_all | solution.py:16
  60.7 15.6 %all-to-all-done.3 = bf16[16,4,4096]{2,1,0:T(4,128)(2,1)S(1)} async-done(((bf16[16,4,4096]{2,1,0:T(4,128)(2,1)}), bf16[16,4,4096]{2,1,0:T(4,128)(2,1)S(1)}, u32[]{:S(2)}, u32[]{:S(2)}) %all-to-all-start.3) | async-done | bytes 524320 | tf_op jit(solution)/shard_map/all_to_all | solution.py:16
  77.5 23.2 %all_to_all.47 = bf16[32,2,4224]{2,1,0:T(2,128)(2,1)S(1)} all-to-all(bf16[32,2,4224]{2,1,0:T(2,128)(2,1)S(1)} %reshape.158), channel_id=1, replica_groups=mesh['zl'=2,'y'=8,'x'=4,'zh'=4,'co'=2] {'x','zh','co'}, dimensions={0} | all-to-all | bytes 1081344 | tf_op jit(solution)/shard_map/all_to_all | solution.py:16
  100.7 1.0 reshape.159
  101.9 1.3 fusion.38
  103.3 5.0 %collective-permute-start = (bf16[2,96,4096]{2,1,0:T(8,128)(2,1)S(1)}, bf16[2,96,4096]{2,1,0:T(8,128)(2,1)S(1)}, u32[]{:S(2)}, u32[]{:S(2)}) collective-permute-start(bf16[2,96,4096]{2,1,0:T(8,128)(2,1)S(1)} %get-tuple-element.7), channel_id=1, source_target_pairs={{0,256},{256,0},{1,257},{257,1},{2,258},{258,2},{3,259},{259,3},{4... | collective-permute-start | bytes 4718600 | tf_op jit(solution)/shard_map/ppermute | solution.py:76
  108.3 34.6 %collective-permute-done = bf16[2,96,4096]{2,1,0:T(8,128)(2,1)S(1)} collective-permute-done((bf16[2,96,4096]{2,1,0:T(8,128)(2,1)S(1)}, bf16[2,96,4096]{2,1,0:T(8,128)(2,1)S(1)}, u32[]{:S(2)}, u32[]{:S(2)}) %collective-permute-start) | collective-permute-done | bytes 1572896 | tf_op jit(solution)/shard_map/ppermute | solution.py:76
  142.9 2.0 fusion.2
  144.9 8.5 %all-gather.2.cloned.1.call-done = bf16[512,4224]{1,0:T(8,128)(2,1)} async-done(((bf16[64,4224]{1,0:T(8,128)(2,1)}), bf16[512,4224]{1,0:T(8,128)(2,1)}) %all-gather.2.cloned.1.call-update) | async-done | bytes 4325392 | tf_op jit(solution)/shard_map/all_gather | solution.py:113
  153.4 5.1 %fusion.40 = f32[384,512]{1,0:T(8,128)S(1)} fusion(bf16[384,4224]{1,0:T(8,128)(2,1)} %bitcast.70, bf16[512,4224]{1,0:T(8,128)(2,1)} %all-gather.2.cloned.1.call-done), kind=kOutput, calls=%fused_computation.80 | convolution fusion | flops 1660944384 | bytes 8355840 | tf_op jit(solution)/shard_map/dot_general | solution.py:28
  158.7 1.3 broadcast_in_dim.31
  160.0 6.4 %all-to-all-start.5 = ((bf16[8,192,512]{2,1,0:T(8,128)(2,1)}), bf16[8,192,512]{2,1,0:T(8,128)(2,1)}, u32[]{:S(2)}, u32[]{:S(2)}) async-start(bf16[8,192,512]{2,1,0:T(8,128)(2,1)} %broadcast_in_dim.31), calls=%async_computation.5 | async-start | bytes 3145728 | tf_op jit(solution)/shard_map/all_to_all | solution.py:16
  166.4 3.5 %collective-permute-start.1 = (bf16[1536,256]{1,0:T(8,128)(2,1)S(1)}, bf16[1536,256]{1,0:T(8,128)(2,1)}, u32[]{:S(2)}, u32[]{:S(2)}) collective-permute-start(bf16[1536,256]{1,0:T(8,128)(2,1)S(1)} %bitcast.78), channel_id=1, source_target_pairs={{0,256},{256,0},{1,257},{257,1},{2,258},{258,2},{3,259},{259,3},{4... | collective-permute-start | bytes 2359304 | tf_op jit(solution)/shard_map/ppermute | solution.py:77
  169.9 17.1 %collective-permute-done.1 = bf16[1536,256]{1,0:T(8,128)(2,1)} collective-permute-done((bf16[1536,256]{1,0:T(8,128)(2,1)S(1)}, bf16[1536,256]{1,0:T(8,128)(2,1)}, u32[]{:S(2)}, u32[]{:S(2)}) %collective-permute-start.1) | collective-permute-done | bytes 786464 | tf_op jit(solution)/shard_map/ppermute | solution.py:77
  187.1 1.3 pad_maximum_fusion.1
  188.7 1.4 copy.86
  190.0 0.9 slice_convert_fusion
  191.4 13.5 %all-to-all-done.5 = bf16[8,192,512]{2,1,0:T(8,128)(2,1)} async-done(((bf16[8,192,512]{2,1,0:T(8,128)(2,1)}), bf16[8,192,512]{2,1,0:T(8,128)(2,1)}, u32[]{:S(2)}, u32[]{:S(2)}) %all-to-all-start.5) | async-done | bytes 1572896 | tf_op jit(solution)/shard_map/all_to_all | solution.py:16
  205.0 4.5 %fusion.10 = bf16[1024,512]{1,0:T(8,128)(2,1)} fusion(s32[512]{0:T(512)S(1)} %fusion.34, s32[1024]{0:T(1024)S(1)} %copy-done.8, bf16[1536,512]{1,0:T(8,128)(2,1)} %bitcast.21, bf16[1536,512]{1,0:T(8,128)(2,1)} %bitcast.73, f32[512]{0:T(512)S(1)} %fusion.23), kind=kOutput, calls=%fused_computation.19 | convolution fusion | flops 1343750144 | bytes 4202496 | tf_op jit(solution)/shard_map/dot_general | solution.py:142
  209.5 5.7 %all_to_all.48 = bf16[2,512,512]{2,1,0:T(8,128)(2,1)S(1)} all-to-all(bf16[2,512,512]{2,1,0:T(8,128)(2,1)} %bitcast.75), channel_id=1, replica_groups=mesh['zl'=2,'y'=8,'x'=4,'zh'=4,'co'=2] {'co'}, dimensions={0} | all-to-all | bytes 2097152 | tf_op jit(solution)/shard_map/all_to_all | solution.py:16
  215.2 1.1 reduce_sum.116
  216.3 14.0 %all_to_all.49 = bf16[4,128,512]{2,1,0:T(8,128)(2,1)S(1)} all-to-all(bf16[4,128,512]{2,1,0:T(8,128)(2,1)} %bitcast.72), channel_id=1, replica_groups=mesh['zl'=2,'y'=8,'x'=4,'zh'=4,'co'=2] {'x'}, dimensions={0} | all-to-all | bytes 1048576 | tf_op jit(solution)/shard_map/all_to_all | solution.py:16
  230.4 20.9 %all_to_all.50 = bf16[32,4,512]{2,1,0:T(4,128)(2,1)S(1)} all-to-all(bf16[32,4,512]{2,1,0:T(4,128)(2,1)S(1)} %reshape.165), channel_id=1, replica_groups=mesh['zl'=2,'y'=8,'x'=4,'zh'=4,'co'=2] {'zh','y'}, dimensions={0} | all-to-all | bytes 262144 | tf_op jit(solution)/shard_map/all_to_all | solution.py:16
  (63 shorter events, 8.0 us)
Async XLA Ops:
  7.2 32.4 %copy-start = (bf16[256,4096]{1,0:T(8,128)(2,1)S(1)}, bf16[256,4096]{1,0:T(8,128)(2,1)}, u32[]{:S(2)}) copy-start(bf16[256,4096]{1,0:T(8,128)(2,1)} %param.17) | copy-start | bytes 6291460
  9.0 24.4 %all-to-all-start = ((bf16[16,128,128]{2,1,0:T(8,128)(2,1)}), bf16[16,128,128]{2,1,0:T(8,128)(2,1)S(1)}, u32[]{:S(2)}, u32[]{:S(2)}) async-start(bf16[16,128,128]{2,1,0:T(8,128)(2,1)} %broadcast_in_dim.21), calls=%async_computation | async-start | bytes 1048576 | tf_op jit(solution)/shard_map/all_to_all | solution.py:16
  44.6 15.2 %copy-start.6 = (s32[4,8]{1,0:T(4,128)S(1)}, s32[4,8]{1,0:T(4,128)}, u32[]{:S(2)}) copy-start(s32[4,8]{1,0:T(4,128)} %param.19) | copy-start | bytes 388
  44.6 15.6 %copy-start.7 = (f32[4,8]{1,0:T(4,128)S(1)}, f32[4,8]{1,0:T(4,128)}, u32[]{:S(2)}) copy-start(f32[4,8]{1,0:T(4,128)} %param.20) | copy-start | bytes 388
  44.6 32.1 %copy-start.4 = (bf16[4,4096]{1,0:T(4,128)(2,1)S(1)}, bf16[4,4096]{1,0:T(4,128)(2,1)}, u32[]{:S(2)}) copy-start(bf16[4,4096]{1,0:T(4,128)(2,1)} %param.16) | copy-start | bytes 98308
  44.6 32.3 %copy-start.5 = (f32[4096]{0:T(1024)S(1)}, f32[4096]{0:T(1024)}, u32[]{:S(2)}) copy-start(f32[4096]{0:T(1024)} %param.18) | copy-start | bytes 49156
  47.8 28.5 %all-to-all-start.3 = ((bf16[16,4,4096]{2,1,0:T(4,128)(2,1)}), bf16[16,4,4096]{2,1,0:T(4,128)(2,1)S(1)}, u32[]{:S(2)}, u32[]{:S(2)}) async-start(bf16[16,4,4096]{2,1,0:T(4,128)(2,1)} %reshape.155), calls=%async_computation.3 | async-start | bytes 1048576 | tf_op jit(solution)/shard_map/all_to_all | solution.py:16
  59.8 93.6 %all-gather.2.cloned.1.call-start = ((), (), s32[]{:S(2)}) async-start(), calls=%async_computation.9 | async-start | bytes 4866048 | tf_op jit(solution)/shard_map/all_gather | solution.py:113
  76.9 24.9 %copy-start.3 = (bf16[4,4096]{1,0:T(4,128)(2,1)}, bf16[4,4096]{1,0:T(4,128)(2,1)S(1)}, u32[]{:S(2)}) copy-start(bf16[4,4096]{1,0:T(4,128)(2,1)S(1)} %get-tuple-element.3) | copy-start | bytes 98308
  100.7 1.2 copy-start.1
  103.3 39.7 %collective-permute-start = (bf16[2,96,4096]{2,1,0:T(8,128)(2,1)S(1)}, bf16[2,96,4096]{2,1,0:T(8,128)(2,1)S(1)}, u32[]{:S(2)}, u32[]{:S(2)}) collective-permute-start(bf16[2,96,4096]{2,1,0:T(8,128)(2,1)S(1)} %get-tuple-element.7), channel_id=1, source_target_pairs={{0,256},{256,0},{1,257},{257,1},{2,258},{258,2},{3,259},{259,3},{4... | collective-permute-start | bytes 4718600 | tf_op jit(solution)/shard_map/ppermute | solution.py:76
  158.7 7.7 %copy-start.2 = (bf16[1,1536,256]{2,1,0:T(8,128)(2,1)S(1)}, bf16[1,1536,256]{2,1,0:T(8,128)(2,1)}, u32[]{:S(2)}) copy-start(bf16[1,1536,256]{2,1,0:T(8,128)(2,1)} %param.23) | copy-start | bytes 2359300
  160.0 45.0 %all-to-all-start.5 = ((bf16[8,192,512]{2,1,0:T(8,128)(2,1)}), bf16[8,192,512]{2,1,0:T(8,128)(2,1)}, u32[]{:S(2)}, u32[]{:S(2)}) async-start(bf16[8,192,512]{2,1,0:T(8,128)(2,1)} %broadcast_in_dim.31), calls=%async_computation.5 | async-start | bytes 3145728 | tf_op jit(solution)/shard_map/all_to_all | solution.py:16
  166.4 20.7 %collective-permute-start.1 = (bf16[1536,256]{1,0:T(8,128)(2,1)S(1)}, bf16[1536,256]{1,0:T(8,128)(2,1)}, u32[]{:S(2)}, u32[]{:S(2)}) collective-permute-start(bf16[1536,256]{1,0:T(8,128)(2,1)S(1)} %bitcast.78), channel_id=1, source_target_pairs={{0,256},{256,0},{1,257},{257,1},{2,258},{258,2},{3,259},{259,3},{4... | collective-permute-start | bytes 2359304 | tf_op jit(solution)/shard_map/ppermute | solution.py:77
  188.7 16.3 %copy-start.8 = (s32[1024]{0:T(1024)S(1)}, s32[1024]{0:T(1024)}, u32[]{:S(2)}) copy-start(s32[1024]{0:T(1024)} %constant.94.clone) | copy-start | bytes 12292
Sparse Core Ops, SparseCore 0:
  101.9 51.4 all-gather.1
where the time goes:
time: 260 us; the launch traced here: 259 us
  waiting for transfers between devices  102 us (39%)
  blocking collectives  73 us (28%)
  starting transfers between devices  36.4 us (14%)
  between operations  14.3 us (6%)
  other arithmetic  11.8 us (5%)
  matrix products  11.5 us (4%)
  local copies, waits for them, and re-layouts  10.4 us (4%)
    all_to_all x6, blocking collectives, exchange(): return lax.all_to_all(pieces, axis, 0, 0, tiled=True)  73 us
    all_to_all x3, waiting for transfers between devices, exchange(): return lax.all_to_all(pieces, axis, 0, 0, tiled=True)  41.5 us
    ppermute x1, waiting for transfers between devices, on_device(): gate_up_other = lax.ppermute(gate_up, 'zl', swap)  34.6 us
    all_to_all x3, starting transfers between devices, exchange(): return lax.all_to_all(pieces, axis, 0, 0, tiled=True)  27.7 us
    ppermute x1, waiting for transfers between devices, on_device(): down_other = lax.ppermute(w_down[0], 'zl', swap)  17.1 us
    all_gather x1, waiting for transfers between devices, on_device(): lax.all_gather(arrived.reshape(expert_count * slots, width + EXTRA), 'y',...  8.52 us
    dot_general x2, matrix products, rows_dot(): lax.dot_general(left, right, (((1,), (1,)), ((), ())), preferred_element_...  5.64 us
  transfers between devices with their start and end apart: 6, of which 6 were waited for; matrix products, arithmetic and copies ran while one was open for 4% of the time, Pallas kernels for 0%

commit v1 on v0

--- a/solution.py
+++ b/solution.py
@@ -10,6 +10,11 @@
 EXP = ("x", "zh", "co")
 EPS_NORM = 1e-06
 NEG_LARGE = -1e30
+
+
+def all_by_exchange(block, name, along):
+    repeated = jnp.stack([block] * lax.axis_size(name))
+    return jnp.concatenate(lax.all_to_all(repeated, name, 0, 0), axis=along)
 
 
 def exchange(pieces, axis):
@@ -110,9 +115,7 @@
     outgoing = jnp.dot(table, normed, preferred_element_type=jnp.float32).astype(jnp.bfloat16)
     outgoing = jnp.concatenate([outgoing, extra], axis=1)
     arrived = exchange(outgoing.reshape(expert_count, slots, width + EXTRA), EXP)
-    rows = lax.all_gather(
-        arrived.reshape(expert_count * slots, width + EXTRA), "y", axis=0, tiled=True
-    )
+    rows = all_by_exchange(arrived.reshape(expert_count * slots, width + EXTRA), "y", 0)
     weight_in = jnp.stack([gate_up, gate_up_other], axis=1)
     weight_in = jnp.pad(weight_in, ((0, 0),) * 3 + ((0, EXTRA),)).reshape(-1, width + EXTRA)
     both = rows_dot(weight_in, rows)

time: 260 us -> 297 us (1.14)
  waiting for transfers between devices: 102 us -> 149 us
  between operations: 14.3 us -> 0.94 us
  local copies, waits for them, and re-layouts: 10.4 us -> 14 us
  starting transfers between devices: 36.4 us -> 39.5 us
    all_to_all x0 -> x1, waiting for transfers between devices: none -> 56.8 us  [all_by_exchange(): return jnp.concatenate(lax.all_to_all(repeated, name, 0, 0), axis=along)]
    all_gather x1 -> x0, waiting for transfers between devices: 8.52 us -> none  [on_device(): lax.all_gather(arrived.reshape(expert_count * slots, width + EXTRA), 'y',...]
    all_to_all x0 -> x1, starting transfers between devices: none -> 7.07 us  [all_by_exchange(): return jnp.concatenate(lax.all_to_all(repeated, name, 0, 0), axis=along)]
    another operation x0 -> x2, local copies, waits for them, and re-layouts: none -> 3.78 us  [all_by_exchange(): repeated = jnp.stack([block] * lax.axis_size(name))]
where the time goes in v1:
time: 297 us; the launch traced here: 296 us
  waiting for transfers between devices  149 us (50%)
  blocking collectives  70.1 us (24%)
  starting transfers between devices  39.5 us (13%)
  local copies, waits for them, and re-layouts  14 us (5%)
  matrix products  11.5 us (4%)
  other arithmetic  10.6 us (4%)
    all_to_all x6, blocking collectives, exchange(): return lax.all_to_all(pieces, axis, 0, 0, tiled=True)  70.1 us
    all_to_all x1, waiting for transfers between devices, all_by_exchange(): return jnp.concatenate(lax.all_to_all(repeated, name, 0, 0), axis=along)  56.8 us
    all_to_all x3, waiting for transfers between devices, exchange(): return lax.all_to_all(pieces, axis, 0, 0, tiled=True)  40 us
    ppermute x1, waiting for transfers between devices, on_device(): gate_up_other = lax.ppermute(gate_up, 'zl', swap)  35.1 us
    all_to_all x3, starting transfers between devices, exchange(): return lax.all_to_all(pieces, axis, 0, 0, tiled=True)  27.1 us
    ppermute x1, waiting for transfers between devices, on_device(): down_other = lax.ppermute(w_down[0], 'zl', swap)  17.5 us
    all_to_all x1, starting transfers between devices, all_by_exchange(): return jnp.concatenate(lax.all_to_all(repeated, name, 0, 0), axis=along)  7.07 us
  transfers between devices with their start and end apart: 6, of which 6 were waited for; matrix products, arithmetic and copies ran while one was open for 4% of the time, Pallas kernels for 0%

profile of v1, /device:TPU:8, one launch (start us, length us, event | category | flops | bytes accessed | tf_op | source)
XLA Modules:
  0.0 296.0 jit_solution(15440763622815049772)
XLA Ops:
  0.7 0.9 dynamic-slice_select_fusion
  2.5 9.4 %all-to-all-start = ((bf16[16,128,128]{2,1,0:T(8,128)(2,1)}), bf16[16,128,128]{2,1,0:T(8,128)(2,1)S(1)}, u32[]{:S(2)}, u32[]{:S(2)}) async-start(bf16[16,128,128]{2,1,0:T(8,128)(2,1)} %broadcast_in_dim.21), calls=%async_computation | async-start | bytes 1048576 | tf_op jit(solution)/shard_map/all_to_all | solution.py:21
  14.5 12.4 %all-to-all-done = bf16[16,128,128]{2,1,0:T(8,128)(2,1)S(1)} async-done(((bf16[16,128,128]{2,1,0:T(8,128)(2,1)}), bf16[16,128,128]{2,1,0:T(8,128)(2,1)S(1)}, u32[]{:S(2)}, u32[]{:S(2)}) %all-to-all-start) | async-done | bytes 524320 | tf_op jit(solution)/shard_map/all_to_all | solution.py:21
  26.9 4.6 %all_to_all.50 = bf16[2,2048,128]{2,1,0:T(8,128)(2,1)S(1)} all-to-all(bf16[2,2048,128]{2,1,0:T(8,128)(2,1)S(1)} %broadcast_in_dim.23), channel_id=1, replica_groups=mesh['zl'=2,'y'=8,'x'=4,'zh'=4,'co'=2] {'co'}, dimensions={0} | all-to-all | bytes 2097152 | tf_op jit(solution)/shard_map/all_to_all | solution.py:21
  33.5 4.6 %all_to_all.51 = bf16[2,64,4096]{2,1,0:T(8,128)(2,1)S(1)} all-to-all(bf16[2,64,4096]{2,1,0:T(8,128)(2,1)S(1)} %bitcast.70), channel_id=1, replica_groups=mesh['zl'=2,'y'=8,'x'=4,'zh'=4,'co'=2] {'co'}, dimensions={0} | all-to-all | bytes 2097152 | tf_op jit(solution)/shard_map/all_to_all | solution.py:21
  38.1 1.1 reduce_sum.109
  39.2 2.0 reshape.157
  41.2 12.0 %all-to-all-start.3 = ((bf16[16,4,4096]{2,1,0:T(4,128)(2,1)}), bf16[16,4,4096]{2,1,0:T(4,128)(2,1)S(1)}, u32[]{:S(2)}, u32[]{:S(2)}) async-start(bf16[16,4,4096]{2,1,0:T(4,128)(2,1)} %reshape.157), calls=%async_computation.3 | async-start | bytes 1048576 | tf_op jit(solution)/shard_map/all_to_all | solution.py:21
  54.1 15.7 %all-to-all-done.3 = bf16[16,4,4096]{2,1,0:T(4,128)(2,1)S(1)} async-done(((bf16[16,4,4096]{2,1,0:T(4,128)(2,1)}), bf16[16,4,4096]{2,1,0:T(4,128)(2,1)S(1)}, u32[]{:S(2)}, u32[]{:S(2)}) %all-to-all-start.3) | async-done | bytes 524320 | tf_op jit(solution)/shard_map/all_to_all | solution.py:21
  71.0 23.3 %all_to_all.52 = bf16[32,2,4224]{2,1,0:T(2,128)(2,1)} all-to-all(bf16[32,2,4224]{2,1,0:T(2,128)(2,1)S(1)} %reshape.160), channel_id=1, replica_groups=mesh['zl'=2,'y'=8,'x'=4,'zh'=4,'co'=2] {'x','zh','co'}, dimensions={0} | all-to-all | bytes 1081344 | tf_op jit(solution)/shard_map/all_to_all | solution.py:21
  94.3 1.3 stack_reshape.2
  95.6 2.5 stack.21
  98.1 7.1 %all-to-all-start.5 = ((bf16[8,64,4224]{2,1,0:T(8,128)(2,1)}), bf16[8,64,4224]{2,1,0:T(8,128)(2,1)}, u32[]{:S(2)}, u32[]{:S(2)}) async-start(bf16[8,64,4224]{2,1,0:T(8,128)(2,1)} %stack.21), calls=%async_computation.5 | async-start | bytes 8650752 | tf_op jit(solution)/shard_map/all_to_all | solution.py:17
  105.2 1.3 fusion.38
  106.5 2.6 collective-permute-start
  109.2 35.1 %collective-permute-done = bf16[2,96,4096]{2,1,0:T(8,128)(2,1)S(1)} collective-permute-done((bf16[2,96,4096]{2,1,0:T(8,128)(2,1)S(1)}, bf16[2,96,4096]{2,1,0:T(8,128)(2,1)S(1)}, u32[]{:S(2)}, u32[]{:S(2)}) %collective-permute-start) | collective-permute-done | bytes 1572896 | tf_op jit(solution)/shard_map/ppermute | solution.py:81
  144.2 2.0 fusion.2
  146.2 56.8 %all-to-all-done.5 = bf16[8,64,4224]{2,1,0:T(8,128)(2,1)} async-done(((bf16[8,64,4224]{2,1,0:T(8,128)(2,1)}), bf16[8,64,4224]{2,1,0:T(8,128)(2,1)}, u32[]{:S(2)}, u32[]{:S(2)}) %all-to-all-start.5) | async-done | bytes 4325408 | tf_op jit(solution)/shard_map/all_to_all | solution.py:17
  203.0 5.1 %fusion.40 = f32[384,512]{1,0:T(8,128)S(1)} fusion(bf16[384,4224]{1,0:T(8,128)(2,1)} %bitcast.71, bf16[512,4224]{1,0:T(8,128)(2,1)} %bitcast.11), kind=kOutput, calls=%fused_computation.79 | convolution fusion | flops 1660944384 | bytes 8355840 | tf_op jit(solution)/shard_map/dot_general | solution.py:33
  208.3 1.3 broadcast_in_dim.31
  209.6 5.8 %all-to-all-start.6 = ((bf16[8,192,512]{2,1,0:T(8,128)(2,1)}), bf16[8,192,512]{2,1,0:T(8,128)(2,1)}, u32[]{:S(2)}, u32[]{:S(2)}) async-start(bf16[8,192,512]{2,1,0:T(8,128)(2,1)} %broadcast_in_dim.31), calls=%async_computation.6 | async-start | bytes 3145728 | tf_op jit(solution)/shard_map/all_to_all | solution.py:21
  215.4 2.7 collective-permute-start.1
  218.1 17.5 %collective-permute-done.1 = bf16[1536,256]{1,0:T(8,128)(2,1)} collective-permute-done((bf16[1536,256]{1,0:T(8,128)(2,1)S(1)}, bf16[1536,256]{1,0:T(8,128)(2,1)}, u32[]{:S(2)}, u32[]{:S(2)}) %collective-permute-start.1) | collective-permute-done | bytes 786464 | tf_op jit(solution)/shard_map/ppermute | solution.py:82
  235.6 1.3 pad_maximum_fusion.1
  237.2 1.4 copy.99
  238.6 0.9 slice.20
  239.7 12.0 %all-to-all-done.6 = bf16[8,192,512]{2,1,0:T(8,128)(2,1)} async-done(((bf16[8,192,512]{2,1,0:T(8,128)(2,1)}), bf16[8,192,512]{2,1,0:T(8,128)(2,1)}, u32[]{:S(2)}, u32[]{:S(2)}) %all-to-all-start.6) | async-done | bytes 1572896 | tf_op jit(solution)/shard_map/all_to_all | solution.py:21
  251.7 4.5 %fusion.10 = bf16[1024,512]{1,0:T(8,128)(2,1)} fusion(s32[512]{0:T(512)S(1)} %fusion.33, s32[1024]{0:T(1024)S(1)} %copy-done.8, bf16[1536,512]{1,0:T(8,128)(2,1)} %bitcast.22, bf16[1536,512]{1,0:T(8,128)(2,1)} %bitcast.74, f32[512]{0:T(512)S(1)} %fusion.37), kind=kOutput, calls=%fused_computation.19 | convolution fusion | flops 1343750144 | bytes 4202496 | tf_op jit(solution)/shard_map/dot_general | solution.py:145
  256.2 5.7 %all_to_all.53 = bf16[2,512,512]{2,1,0:T(8,128)(2,1)S(1)} all-to-all(bf16[2,512,512]{2,1,0:T(8,128)(2,1)} %bitcast.76), channel_id=1, replica_groups=mesh['zl'=2,'y'=8,'x'=4,'zh'=4,'co'=2] {'co'}, dimensions={0} | all-to-all | bytes 2097152 | tf_op jit(solution)/shard_map/all_to_all | solution.py:21
  261.9 1.1 reduce_sum.116
  263.0 15.6 %all_to_all.54 = bf16[4,128,512]{2,1,0:T(8,128)(2,1)S(1)} all-to-all(bf16[4,128,512]{2,1,0:T(8,128)(2,1)} %bitcast.73), channel_id=1, replica_groups=mesh['zl'=2,'y'=8,'x'=4,'zh'=4,'co'=2] {'x'}, dimensions={0} | all-to-all | bytes 1048576 | tf_op jit(solution)/shard_map/all_to_all | solution.py:21
  278.8 16.3 %all_to_all.55 = bf16[32,4,512]{2,1,0:T(4,128)(2,1)S(1)} all-to-all(bf16[32,4,512]{2,1,0:T(4,128)(2,1)S(1)} %reshape.167), channel_id=1, replica_groups=mesh['zl'=2,'y'=8,'x'=4,'zh'=4,'co'=2] {'zh','y'}, dimensions={0} | all-to-all | bytes 262144 | tf_op jit(solution)/shard_map/all_to_all | solution.py:21
  (65 shorter events, 9.3 us)
Async XLA Ops:
  0.6 32.4 %copy-start = (bf16[256,4096]{1,0:T(8,128)(2,1)S(1)}, bf16[256,4096]{1,0:T(8,128)(2,1)}, u32[]{:S(2)}) copy-start(bf16[256,4096]{1,0:T(8,128)(2,1)} %param.17) | copy-start | bytes 6291460
  2.5 24.4 %all-to-all-start = ((bf16[16,128,128]{2,1,0:T(8,128)(2,1)}), bf16[16,128,128]{2,1,0:T(8,128)(2,1)S(1)}, u32[]{:S(2)}, u32[]{:S(2)}) async-start(bf16[16,128,128]{2,1,0:T(8,128)(2,1)} %broadcast_in_dim.21), calls=%async_computation | async-start | bytes 1048576 | tf_op jit(solution)/shard_map/all_to_all | solution.py:21
  38.1 15.2 %copy-start.6 = (s32[4,8]{1,0:T(4,128)S(1)}, s32[4,8]{1,0:T(4,128)}, u32[]{:S(2)}) copy-start(s32[4,8]{1,0:T(4,128)} %param.19) | copy-start | bytes 388
  38.1 15.6 %copy-start.7 = (f32[4,8]{1,0:T(4,128)S(1)}, f32[4,8]{1,0:T(4,128)}, u32[]{:S(2)}) copy-start(f32[4,8]{1,0:T(4,128)} %param.20) | copy-start | bytes 388
  38.1 32.1 %copy-start.4 = (bf16[4,4096]{1,0:T(4,128)(2,1)S(1)}, bf16[4,4096]{1,0:T(4,128)(2,1)}, u32[]{:S(2)}) copy-start(bf16[4,4096]{1,0:T(4,128)(2,1)} %param.16) | copy-start | bytes 98308
  38.1 32.3 %copy-start.5 = (f32[4096]{0:T(1024)S(1)}, f32[4096]{0:T(1024)}, u32[]{:S(2)}) copy-start(f32[4096]{0:T(1024)} %param.18) | copy-start | bytes 49156
  41.2 28.5 %all-to-all-start.3 = ((bf16[16,4,4096]{2,1,0:T(4,128)(2,1)}), bf16[16,4,4096]{2,1,0:T(4,128)(2,1)S(1)}, u32[]{:S(2)}, u32[]{:S(2)}) async-start(bf16[16,4,4096]{2,1,0:T(4,128)(2,1)} %reshape.157), calls=%async_computation.3 | async-start | bytes 1048576 | tf_op jit(solution)/shard_map/all_to_all | solution.py:21
  70.3 25.2 %copy-start.3 = (bf16[4,4096]{1,0:T(4,128)(2,1)}, bf16[4,4096]{1,0:T(4,128)(2,1)S(1)}, u32[]{:S(2)}) copy-start(bf16[4,4096]{1,0:T(4,128)(2,1)S(1)} %get-tuple-element.3) | copy-start | bytes 98308
  98.1 7.1 %copy-start.1 = (bf16[1,4096,96]{1,2,0:T(8,128)(2,1)S(1)}, bf16[1,4096,96]{1,2,0:T(8,128)(2,1)}, u32[]{:S(2)}) copy-start(bf16[1,4096,96]{1,2,0:T(8,128)(2,1)} %param.22) | copy-start | bytes 2359300
  98.1 104.9 %all-to-all-start.5 = ((bf16[8,64,4224]{2,1,0:T(8,128)(2,1)}), bf16[8,64,4224]{2,1,0:T(8,128)(2,1)}, u32[]{:S(2)}, u32[]{:S(2)}) async-start(bf16[8,64,4224]{2,1,0:T(8,128)(2,1)} %stack.21), calls=%async_computation.5 | async-start | bytes 8650752 | tf_op jit(solution)/shard_map/all_to_all | solution.py:17
  106.5 37.7 %collective-permute-start = (bf16[2,96,4096]{2,1,0:T(8,128)(2,1)S(1)}, bf16[2,96,4096]{2,1,0:T(8,128)(2,1)S(1)}, u32[]{:S(2)}, u32[]{:S(2)}) collective-permute-start(bf16[2,96,4096]{2,1,0:T(8,128)(2,1)S(1)} %get-tuple-element.7), channel_id=1, source_target_pairs={{0,256},{256,0},{1,257},{257,1},{2,258},{258,2},{3,259},{259,3},{4... | collective-permute-start | bytes 4718600 | tf_op jit(solution)/shard_map/ppermute | solution.py:81
  208.3 7.1 %copy-start.2 = (bf16[1,1536,256]{2,1,0:T(8,128)(2,1)S(1)}, bf16[1,1536,256]{2,1,0:T(8,128)(2,1)}, u32[]{:S(2)}) copy-start(bf16[1,1536,256]{2,1,0:T(8,128)(2,1)} %param.23) | copy-start | bytes 2359300
  209.6 42.1 %all-to-all-start.6 = ((bf16[8,192,512]{2,1,0:T(8,128)(2,1)}), bf16[8,192,512]{2,1,0:T(8,128)(2,1)}, u32[]{:S(2)}, u32[]{:S(2)}) async-start(bf16[8,192,512]{2,1,0:T(8,128)(2,1)} %broadcast_in_dim.31), calls=%async_computation.6 | async-start | bytes 3145728 | tf_op jit(solution)/shard_map/all_to_all | solution.py:21
  215.4 20.2 %collective-permute-start.1 = (bf16[1536,256]{1,0:T(8,128)(2,1)S(1)}, bf16[1536,256]{1,0:T(8,128)(2,1)}, u32[]{:S(2)}, u32[]{:S(2)}) collective-permute-start(bf16[1536,256]{1,0:T(8,128)(2,1)S(1)} %bitcast.79), channel_id=1, source_target_pairs={{0,256},{256,0},{1,257},{257,1},{2,258},{258,2},{3,259},{259,3},{4... | collective-permute-start | bytes 2359304 | tf_op jit(solution)/shard_map/ppermute | solution.py:82
  237.2 14.5 %copy-start.8 = (s32[1024]{0:T(1024)S(1)}, s32[1024]{0:T(1024)}, u32[]{:S(2)}) copy-start(s32[1024]{0:T(1024)} %constant.94.clone) | copy-start | bytes 12292
